TPU v7x, 128 devices: a whole 4x4x4 slice. The times are simulated.
128 devices in a mesh: lat: 8 (over z_hi, x), lon: 16 (over z_lo, y, core).
Axes of the slice: x: 4, y: 4, z: 4 (z_hi: 2, z_lo: 2; z = z_hi * 2 + z_lo), core: 2. Of those that a mesh axis runs over, the one named last changes fastest.
Arguments:
- tokens: bfloat16 [512, 256, 512], P('lat', 'lon'), may hold values from -8 to 8
- region: int32 [512, 256], P('lat', 'lon'), may hold values from 0 to 2
- qkv_one: bfloat16 [512, 1536], replicated, may hold values from -6 to 6
- proj_one: bfloat16 [512, 512], replicated, may hold values from -0.25 to 0.25
- merge_weight: bfloat16 [2048, 1024], replicated, may hold values from -0.125 to 0.125
- qkv_two: bfloat16 [1024, 3072], replicated, may hold values from -6 to 6
- proj_two: bfloat16 [1024, 1024], replicated, may hold values from -0.1875 to 0.1875
- unmerge_weight: bfloat16 [1024, 2048], replicated, may hold values from -0.1875 to 0.1875
- cotangent: bfloat16 [512, 256, 512], P('lat', 'lon'), may hold values from -6 to 6
Outputs:
- output: bfloat16 [512, 256, 512], P('lat', 'lon')
- grad_tokens: bfloat16 [512, 256, 512], P('lat', 'lon')
- grad_qkv_two: float32 [1024, 3072], P(('lat', 'lon'))
- grad_proj_two: float32 [1024, 1024], P(('lat', 'lon'))
Inputs may be any that keep to these rules, and one draw needn't show every extreme that they name: `region`: labels compared within a window of the shifted grid.
All inputs are finite; a program needn't handle non-finite values.
Results may differ from a plain program's by a relative error of at most 0.028.
Values may be sent and summed in bfloat16 or wider, within the bound.
A program may use at most 192 MiB of HBM per device.

v0:
```python
import itertools
from types import SimpleNamespace

import jax
import jax.numpy as jnp
from jax import lax
from jax.experimental import pallas as pl
from jax.experimental.pallas import tpu as pltpu
from jax.sharding import PartitionSpec as P

MESH = pl.DeviceIdType.MESH
BF = jnp.bfloat16
F32 = jnp.float32
VMEM_LIMIT = 63 * 1024 * 1024

TOKENS, C1, C2 = 1024, 512, 1024
COARSE = 256
LONS, LATS = 16, 8

FOLD = 2048
PARTS = ((0, 640, ("x", "y", "z")), (640, 1280, ("y", "z", "x")), (1280, 2048, ("z", "x", "y")))
LABELS = ("zh", "x", "zl", "y")


def coordinates():
    lat, lon = lax.axis_index("lat"), lax.axis_index("lon")
    return {
        "zh": lat // 4,
        "x": lat % 4,
        "zl": lon // 8,
        "y": (lon // 2) % 4,
        "core": lon % 2,
    }


def device_of(c):
    return (c["zh"] * 4 + c["x"], (c["zl"] * 4 + c["y"]) * 2 + c["core"])


def moved(c, axis, by):
    c = dict(c)
    if axis == "z":
        z = (c["zh"] * 2 + c["zl"] + by) % 4
        c["zh"], c["zl"] = z // 2, z % 2
    elif axis == "core":
        c["core"] = 1 - c["core"]
    else:
        c[axis] = (c[axis] + by) % 4
    return c


def pick(labels, axis, c):
    names = ("zh", "zl") if axis == "z" else (axis,)
    return tuple(c[label] if label in names else slice(None) for label in labels)


def drop(labels, axis):
    names = ("zh", "zl") if axis == "z" else (axis,)
    return tuple(label for label in labels if label not in names)


def sizes(labels):
    return tuple(4 if label in ("x", "y") else 2 for label in labels)


def remote(source, target, send_sem, recv_sem, device):
    return pltpu.make_async_remote_copy(
        src_ref=source,
        dst_ref=target,
        send_sem=send_sem,
        recv_sem=recv_sem,
        device_id=device,
        device_id_type=MESH,
    )


def reduce_scratch():
    shapes = [pltpu.VMEM((2, 4, 2, 4, 16, FOLD), BF)]
    for start, stop, order in PARTS:
        labels = LABELS
        for step, axis in enumerate(order):
            labels = drop(labels, axis)
            shapes.append(pltpu.VMEM((3,) + sizes(labels) + (16, stop - start), BF))
            if step < 2:
                shapes.append(pltpu.VMEM(sizes(labels) + (16, stop - start), BF))
    return shapes + [pltpu.SemaphoreType.DMA((3, 3, 3)), pltpu.SemaphoreType.DMA((3, 3, 3))]


class Reducer:
    def __init__(self, scratch):
        self.total = scratch[0]
        self.slots = [scratch[1 + 5 * p : 6 + 5 * p] for p in range(3)]
        self.send_sem, self.recv_sem = scratch[16], scratch[17]
        self.c = coordinates()

    def source(self, part, step):
        start, stop, order = PARTS[part]
        labels = LABELS
        for axis in order[:step]:
            labels = drop(labels, axis)
        if step == 0:
            return labels, self.total, (slice(None), pl.ds(start, stop - start))
        return labels, self.slots[part][2 * step - 1], (slice(None), slice(None))

    def copies(self, part, step):
        axis = PARTS[part][2][step]
        labels, source, rest = self.source(part, step)
        found = []
        for by in (2, 1, 3):
            target = moved(self.c, axis, by)
            found.append(
                remote(
                    source.at[pick(labels, axis, target) + rest],
                    self.slots[part][2 * step].at[by - 1],
                    self.send_sem.at[part, step, by - 1],
                    self.recv_sem.at[part, step, by - 1],
                    device_of(target),
                )
            )
        return found

    def start(self, part, step):
        for copy in self.copies(part, step):
            copy.start()

    def finish(self, part, step):
        for copy in self.copies(part, step):
            copy.wait_recv()
        axis = PARTS[part][2][step]
        labels, source, rest = self.source(part, step)
        arrived = self.slots[part][2 * step]
        left = drop(labels, axis)
        for place in itertools.product(*[range(size) for size in sizes(left)]):
            where = dict(zip(left, place))
            where.update({k: self.c[k] for k in labels if k not in where})
            own = source[tuple(where[label] for label in labels) + rest].astype(F32)
            summed = own
            for slot in range(3):
                summed = summed + arrived[(slot,) + place].astype(F32)
            if step == 2:
                return summed
            self.slots[part][2 * step + 1][place] = summed.astype(BF)

    def drain(self):
        for part in range(3):
            for step in range(3):
                for copy in self.copies(part, step):
                    copy.wait_send()


def store_folded(part, summed, qkv_ref, proj_ref):
    start, stop, _ = PARTS[part]
    top, low = summed[:8], summed[8:]
    qkv_ref[:, start:stop] = top
    cut = min(max(1024 - start, 0), stop - start)
    if cut:
        qkv_ref[:, FOLD + start : FOLD + start + cut] = low[:, :cut]
    if cut < stop - start:
        proj_ref[:, start + cut - 1024 : stop - 1024] = low[:, cut:]


def block(at, size):
    return pl.ds(pl.multiple_of(at * size, size), size)


def loop(count, body):
    def step(at, carry):
        body(at)
        return carry

    lax.fori_loop(0, count, step, 0)


def dot(a, b):
    return jnp.dot(a, b, preferred_element_type=F32)


def dot_nt(a, b):
    return lax.dot_general(a, b, (((1,), (1,)), ((), ())), preferred_element_type=F32)


def dot_tn(a, b):
    return lax.dot_general(a, b, (((0,), (0,)), ((), ())), preferred_element_type=F32)


def normalised(x):
    centered = x - jnp.mean(x, axis=-1, keepdims=True)
    spread = jnp.mean(centered * centered, axis=-1, keepdims=True)
    scale = lax.rsqrt(spread + 1e-05)
    return centered * scale, scale


def norm_back(x, g):
    hat, scale = normalised(x)
    return scale * (
        g - jnp.mean(g, axis=-1, keepdims=True) - hat * jnp.mean(g * hat, axis=-1, keepdims=True)
    )


def by_head(pair, scale=1.0):
    lane = lax.broadcasted_iota(jnp.int32, (1, 128), 1)
    first = jnp.where(lane < 64, scale, 0.0).astype(BF)
    second = jnp.where(lane < 64, 0.0, scale).astype(BF)
    return jnp.concatenate([pair * first, pair * second], axis=0)


def side_by_side(stacked):
    return jnp.concatenate([stacked[:128], stacked[128:]], axis=1)


def attend(units, allowed):
    ones = by_head(jnp.ones((128, 128), BF))
    scores = [dot_nt(by_head(q, 0.125), k) for q, k, _ in units]
    if allowed is not None:
        scores = [
            jnp.where(allowed[None], one.reshape(2, 128, 128), -1e30).reshape(256, 128)
            for one in scores
        ]
    expo = [jnp.exp(one - jnp.max(one, axis=-1, keepdims=True)).astype(BF) for one in scores]
    found = []
    for one, (_, _, v) in zip(expo, units):
        both = dot(side_by_side(one), jnp.concatenate([by_head(v), ones], axis=1))
        over = 1.0 / both[:, 128:]
        found.append((one, over.astype(BF), (both[:, :128] * over).astype(BF)))
    return found


def attend_back(units):
    minus = jnp.full((128, 128), -1.0, BF)
    found = []
    for q, k, v, expo, over, mixed, g in units:
        g = g * over
        both = by_head(g)
        change = dot_nt(
            jnp.concatenate([both, by_head(g * mixed)], axis=1),
            jnp.concatenate([v, minus], axis=1),
        )
        grad_scores = (expo.astype(F32) * change).astype(BF)
        grad_q = dot(side_by_side(grad_scores), by_head(k, 0.125))
        grad_k = dot_tn(grad_scores, by_head(q, 0.125))
        grad_v = dot_tn(expo, both)
        found.append((grad_q.astype(BF), grad_k.astype(BF), grad_v.astype(BF)))
    return found


def pack_columns(rows):
    n = rows.shape[0] // 32
    width = rows.shape[1]
    late = rows.reshape(n, 2, 16, width)[:, :, 8:, :]
    place = lax.broadcasted_iota(jnp.int32, (n, 8, width), 1)
    both = jnp.where(place < 4, pltpu.roll(late[:, 0], 4, 1), late[:, 1])
    return both.reshape(n * 8, width).astype(BF)


def put_columns(rows, packed):
    n = rows.shape[0] // 32
    width = rows.shape[1]
    pairs = rows.reshape(n, 2, 16, width)
    arrived = packed.astype(F32).reshape(n, 8, width)
    place = lax.broadcasted_iota(jnp.int32, (n, 8, width), 1)
    even = jnp.where(place >= 4, pltpu.roll(arrived, 4, 1), pairs[:, 0, 8:])
    odd = jnp.where(place >= 4, arrived, pairs[:, 1, 8:])
    whole = jnp.concatenate([pairs[:, 0, :8], even, pairs[:, 1, :8], odd], axis=1)
    return whole.reshape(n * 32, width)


class Halo:

    def __init__(self, field, scratch, way, start=0):
        self.field, self.first = field, start
        self.packed, self.columns, self.rows, self.send_sem, self.recv_sem = scratch
        self.way = way

    def pack(self, half):
        def body(at):
            at = at + 4 * half
            rows = self.field[pl.ds(pl.multiple_of(at * 128 + self.first, 64), 128)]
            self.packed[block(at, 32)] = pack_columns(rows.astype(F32))

        loop(4, body)

    def copies(self):
        lat, lon = lax.axis_index("lat"), lax.axis_index("lon")
        way = self.way
        lat_to, lon_to = (lat + way) % LATS, (lon + way) % LONS
        if way == 1:
            plan = (
                (self.field.at[self.first + 960 : self.first + 1024], self.rows.at[:], (lat_to, lon)),
                (self.packed.at[240:256], self.columns.at[0:16], (lat_to, lon_to)),
                (self.packed.at[0:128], self.columns.at[16:144], (lat, lon_to)),
                (self.packed.at[128:240], self.columns.at[144:256], (lat, lon_to)),
            )
        else:
            plan = (
                (self.field.at[0:64], self.rows.at[:], (lat_to, lon)),
                (self.packed.at[0:16], self.columns.at[240:256], (lat_to, lon_to)),
                (self.packed.at[16:128], self.columns.at[0:112], (lat, lon_to)),
                (self.packed.at[128:256], self.columns.at[112:240], (lat, lon_to)),
            )
        return [
            remote(source, target, self.send_sem.at[k], self.recv_sem.at[k], device)
            for k, (source, target, device) in enumerate(plan)
        ]

    def start(self, which):
        copies = self.copies()
        for k in which:
            copies[k].start()

    def wait(self, which):
        copies = self.copies()
        for k in which:
            copies[k].wait_recv()

    def drain(self):
        for copy in self.copies():
            copy.wait_send()

    def assemble(self, part, write):
        if self.way == 1:
            if part == 0:
                write(0, put_columns(self.rows[...].astype(F32), self.columns[0:16]))

            def patch(at):
                at = at + 8 * part
                rows = self.field[pl.ds(pl.multiple_of(at * 64 + self.first, 64), 64)]
                write(at + 1, put_columns(rows.astype(F32), self.columns[block(at + 1, 16)]))

            loop(7 if part else 8, patch)
        else:
            if part == 0:
                write(15, put_columns(self.rows[...].astype(F32), self.columns[240:256]))

            def patch(at):
                at = at + 7 * part
                rows = self.field[block(at + 1, 64)]
                write(at, put_columns(rows.astype(F32), self.columns[block(at, 16)]))

            loop(8 if part else 7, patch)


def halo_scratch():
    return [
        pltpu.VMEM((256, C1), BF),
        pltpu.VMEM((256, C1), BF),
        pltpu.VMEM((64, C1), BF),
        pltpu.SemaphoreType.DMA((4,)),
        pltpu.SemaphoreType.DMA((4,)),
    ]


class Rows:

    def __init__(self, source, target, sems):
        self.source, self.target = source, target
        self.send_sem, self.recv_sem = sems

    def copy(self, by):
        lat, lon = lax.axis_index("lat"), lax.axis_index("lon")
        to = (lon + by) % LONS
        return remote(
            self.source.at[block(to, 16)],
            self.target.at[block(lon, 16)],
            self.send_sem.at[by],
            self.recv_sem.at[by],
            (lat, to),
        )

    def start(self):
        loop(15, lambda at: self.copy(at + 1).start())
        lon = lax.axis_index("lon")
        self.target[block(lon, 16)] = self.source[block(lon, 16)]

    def wait(self):
        loop(15, lambda at: self.copy(at + 1).wait_recv())

    def drain(self):
        loop(15, lambda at: self.copy(at + 1).wait_send())


def spread_lanes(ref, at, rows):
    for k in range(4):
        ref[k, block(at, 64)] = rows[:, 128 * k : 128 * k + 128]


def fine_pieces(ref, at):
    found = {}
    for b in range(2):
        lanes = [ref[k, pl.ds(at * 64 + b, 32, 2), :] for k in range(4)]
        rows = jnp.concatenate(lanes, axis=1).reshape(2, 2, 8, C1)
        for a in range(2):
            found[a, b] = rows[:, a].reshape(16, C1)
    return [found[a, b] for a in range(2) for b in range(2)]


def put_pieces(ref, at, pieces):
    for b in range(2):
        rows = jnp.stack(
            [pieces[b].reshape(2, 8, C1), pieces[2 + b].reshape(2, 8, C1)], axis=1
        ).reshape(32, C1)
        for k in range(4):
            ref[k, pl.ds(at * 64 + b, 32, 2), :] = rows[:, 128 * k : 128 * k + 128]


def joined_rows(ref, at, width):
    return jnp.concatenate([ref[k, block(at, 64)] for k in range(4)], axis=1)


def by_row(x, width):
    x = x.reshape(-1, 2, 8, width)
    return x[:, 0], x[:, 1]


WEIGHTS = dict(
    unmerge=(C2, 4 * C1),
    qkv_one=(C1, 3 * C1),
    proj_one=(C1, C1),
    merge=(4 * C1, C2),
    qkv_two=(C2, 3 * C2),
    proj_two=(C2, C2),
)

BUFFERS = dict(
    window=((TOKENS + 64, C1), BF),
    labels=((8, 128), F32),
    normed_one=((TOKENS, C1), BF),
    packed_one=((TOKENS, 3 * C1), BF),
    expo_one=((32, 256, 128), BF),
    over_one=((32, 128, 128), BF),
    mixed_one=((TOKENS, C1), BF),
    y_shift=((TOKENS, C1), BF),
    grads=((TOKENS, C1), BF),
    outgoing=((TOKENS, C1), BF),
    fine=((COARSE, 4 * C1), BF),
    spare=((4, TOKENS, 128), F32),
    grouped=((COARSE, 4 * C1), BF),
    coarse=((COARSE, C2), BF),
    coarse_rows=((COARSE, C2), BF),
    grad_skip=((COARSE, C2), BF),
    grad_skip_rows=((COARSE, C2), BF),
    normed_two=((COARSE, C2), BF),
    packed_two=((COARSE, 3 * C2), BF),
    expo_two=((16, 256, 128), BF),
    over_two=((16, 128, 128), BF),
    mixed_two=((COARSE, C2), BF),
    grad_mixed_two=((COARSE, C2), BF),
    wide=((COARSE, C2), F32),
    level_two_rows=((COARSE, C2), BF),
    level_two=((COARSE, C2), BF),
    grad_coarse_rows=((COARSE, C2), BF),
    grad_coarse=((COARSE, C2), BF),
    left_q=((512, 512), BF),
    left_p=((512, 512), BF),
    leave=((2, 512, 256), BF),
    right_q=((2 * COARSE, 3 * C2), BF),
    right_p=((2 * COARSE, C2), BF),
)


def scratch_list():
    shapes = [pltpu.VMEM(shape, BF) for shape in WEIGHTS.values()]
    shapes += [pltpu.VMEM(shape, dtype) for shape, dtype in BUFFERS.values()]
    shapes += [pltpu.SemaphoreType.DMA((len(WEIGHTS),)), pltpu.SemaphoreType.DMA((5,))]
    shapes += [pltpu.SemaphoreType.DMA((4,)), pltpu.SemaphoreType.DMA((4,))]
    shapes += [pltpu.SemaphoreType.DMA((LONS,)) for _ in range(8)]
    for _ in range(4):
        shapes += halo_scratch()
    return shapes + reduce_scratch()


def whole_kernel(*refs):
    region, tokens, cotangent = refs[:3]
    stored = refs[3:9]
    out_ref, grad_ref, qkv_ref, proj_ref = refs[9:13]
    scratch = list(refs[13:])

    def take(count):
        taken = scratch[:count]
        del scratch[:count]
        return taken

    weight = SimpleNamespace(**dict(zip(WEIGHTS, take(len(WEIGHTS)))))
    buf = SimpleNamespace(**dict(zip(BUFFERS, take(len(BUFFERS)))))
    load_sem, field_sem = take(2)
    pair_send, pair_recv = take(2)
    row_sems = [take(2) for _ in range(4)]
    halos = [take(5) for _ in range(4)]
    reducer = Reducer(take(len(reduce_scratch())))
    c = reducer.c
    lat, lon = lax.axis_index("lat"), lax.axis_index("lon")

    partners = [(lat, (lon + by) % LONS) for by in range(1, LONS)]
    for way in (1, -1):
        partners.append(((lat + way) % LATS, lon))
        partners.append(((lat + way) % LATS, (lon + way) % LONS))
    partners += [device_of(moved(c, axis, by)) for axis in ("x", "y", "z") for by in (1, 2, 3)]
    barrier = pltpu.get_barrier_semaphore()
    for partner in partners:
        pl.semaphore_signal(barrier, inc=1, device_id=partner, device_id_type=MESH)

    loads = {
        name: pltpu.make_async_copy(source, getattr(weight, name), load_sem.at[k])
        for k, (name, source) in enumerate(zip(WEIGHTS, stored))
    }
    token_load = pltpu.make_async_copy(tokens, buf.window.at[64:1088], field_sem.at[0])
    cotangent_load = pltpu.make_async_copy(cotangent, buf.mixed_one, field_sem.at[1])
    cotangent_again = pltpu.make_async_copy(cotangent, buf.y_shift, field_sem.at[2])
    output_store = pltpu.make_async_copy(buf.outgoing, out_ref, field_sem.at[3])
    grad_store = pltpu.make_async_copy(buf.outgoing, grad_ref, field_sem.at[4])
    token_load.start()
    cotangent_load.start()
    for copy in loads.values():
        copy.start()
    loads = SimpleNamespace(**loads)

    column = lax.broadcasted_iota(jnp.int32, (16, 128), 0)
    place = lax.broadcasted_iota(jnp.int32, (16, 128), 1) & 15
    chosen = jnp.where(column == ((place + 4) & 15), 1.0, 0.0).astype(BF)
    spread_region = dot_tn(region[...].astype(F32).astype(BF), chosen).reshape(8, 8, 128)
    row = lax.broadcasted_iota(jnp.int32, (8, 8, 128), 1)
    token = lax.broadcasted_iota(jnp.int32, (8, 8, 128), 2)
    own_row = jnp.where(row == (token >> 4), spread_region, 0.0)
    second = jnp.where(((token + 4) & 15) >= 8, 1.0, 0.0)[:, 0]
    buf.labels[...] = jnp.sum(own_row, axis=1) * 2.0 + second

    tokens_in = Halo(buf.window, halos[0], 1, 64)
    fine_back = Halo(buf.y_shift, halos[1], -1)
    grads_in = Halo(buf.normed_one, halos[2], 1)
    grads_back = Halo(buf.y_shift, halos[3], -1)
    skip_to_rows = Rows(buf.grad_skip, buf.grad_skip_rows, row_sems[0])
    coarse_to_rows = Rows(buf.coarse, buf.coarse_rows, row_sems[1])
    level_to_tile = Rows(buf.level_two_rows, buf.level_two, row_sems[2])
    grad_to_tile = Rows(buf.grad_coarse_rows, buf.grad_coarse, row_sems[3])

    with jax.named_scope("tokens_in"):
        token_load.wait()
        tokens_in.pack(0)
        tokens_in.pack(1)
        pl.semaphore_wait(barrier, len(partners))
        tokens_in.start(range(4))

    with jax.named_scope("grad_skip"):
        cotangent_load.wait()

        def spread(at):
            spread_lanes(buf.spare, at, buf.mixed_one[block(at, 64)].astype(F32))

        loop(16, spread)

        def group_cotangent(at):
            buf.grouped[block(at, 16)] = jnp.concatenate(
                fine_pieces(buf.spare, at), axis=1
            ).astype(BF)

        loop(16, group_cotangent)
        loads.unmerge.wait()

        def grad_skip(at):
            buf.grad_skip[:, block(at, 256)] = dot_nt(
                buf.grouped[...], weight.unmerge[block(at, 256)]
            ).astype(BF)

        loop(4, grad_skip)
        skip_to_rows.start()

    def lanes(third, pair):
        return slice(C1 * third + 128 * pair, C1 * third + 128 * pair + 128)

    def windows_allowed(group):
        row = jnp.broadcast_to(buf.labels[pl.ds(group, 1), :], (128, 128))
        return row == row.T

    with jax.named_scope("level_one"):
        def write_window(at, rows):
            buf.window[block(at, 64)] = rows.astype(BF)
            buf.normed_one[block(at, 64)] = normalised(rows)[0].astype(BF)

        loads.qkv_one.wait()
        loads.proj_one.wait()
        for half in range(2):
            tokens_in.wait((3,) if half else (0, 1, 2))
            tokens_in.assemble(half, write_window)
            rows = slice(512 * half, 512 * half + 512)

            def project(at):
                buf.packed_one[rows, block(at, 256)] = dot(
                    buf.normed_one[rows], weight.qkv_one[:, block(at, 256)]
                ).astype(BF)

            loop(6, project)

            def attend_group(at):
                group = at + 4 * half
                where = block(group, 128)
                units = [
                    [buf.packed_one[where, lanes(third, pair)] for third in range(3)]
                    for pair in range(4)
                ]
                for pair, found in enumerate(attend(units, windows_allowed(group))):
                    at_unit = group * 4 + pair
                    buf.expo_one[at_unit], buf.over_one[at_unit], mixed = found
                    buf.mixed_one[where, lanes(0, pair)] = mixed

            loop(4, attend_group)

            def add_tokens(at):
                columns = block(at, 256)
                buf.y_shift[rows, columns] = (
                    buf.window[rows, columns].astype(F32)
                    + dot(buf.mixed_one[rows], weight.proj_one[:, columns])
                ).astype(BF)

            loop(2, add_tokens)
            fine_back.pack(half)
            fine_back.start((0, 1, 2) if half == 0 else (3,))

    with jax.named_scope("merge"):
        def write_fine(at, rows):
            spread_lanes(buf.spare, at, rows.astype(BF).astype(F32))

        fine_back.wait((0, 1, 2))
        fine_back.assemble(0, write_fine)
        fine_back.wait((3,))
        fine_back.assemble(1, write_fine)

        def group_fine(at):
            whole = jnp.concatenate(fine_pieces(buf.spare, at), axis=1)
            buf.fine[block(at, 16)] = whole.astype(BF)
            buf.grouped[block(at, 16)] = normalised(whole)[0].astype(BF)

        loop(16, group_fine)
        loads.merge.wait()

        def merge(at):
            columns = block(at, 256)
            buf.coarse[:, columns] = dot(
                buf.grouped[...], weight.merge[:, columns]
            ).astype(BF)

        loop(4, merge)
        coarse_to_rows.start()
        fine_back.drain()
        cotangent_again.start()

    with jax.named_scope("level_two"):
        loads.qkv_two.wait()
        loads.proj_two.wait()
        coarse_to_rows.wait()

        def norm_two(at):
            both = by_row(buf.coarse_rows[block(at, 64)].astype(F32), C2)
            for row in range(2):
                x = both[row].reshape(32, C2)
                where = pl.ds(pl.multiple_of(at * 32 + 128 * row, 32), 32)
                buf.wide[where] = x
                buf.normed_two[where] = normalised(x)[0].astype(BF)

        loop(4, norm_two)

        def project_two(at):
            columns = block(at, 256)
            buf.packed_two[:, columns] = dot(
                buf.normed_two[...], weight.qkv_two[:, columns]
            ).astype(BF)

        loop(12, project_two)

        def operands_two(row, pair):
            rows = slice(128 * row, 128 * row + 128)
            return [
                buf.packed_two[rows, pl.ds(pl.multiple_of(C2 * third + pair * 128, 128), 128)]
                for third in range(3)
            ]

        def attend_two(at):
            places = [(2 * at + k, row) for k in range(2) for row in range(2)]
            units = [operands_two(row, pair) for pair, row in places]
            for (pair, row), found in zip(places, attend(units, None)):
                at_unit = pair * 2 + row
                buf.expo_two[at_unit], buf.over_two[at_unit], mixed = found
                buf.mixed_two[128 * row : 128 * row + 128, block(pair, 128)] = mixed

        loop(4, attend_two)

        def add_coarse(at):
            columns = block(at, 256)
            total = buf.wide[:, columns] + dot(buf.mixed_two[...], weight.proj_two[:, columns])
            buf.level_two_rows[:, columns] = (
                jnp.stack([total[:128].reshape(16, 8, 256), total[128:].reshape(16, 8, 256)], axis=1)
                .reshape(256, 256)
                .astype(BF)
            )

        loop(4, add_coarse)
        level_to_tile.start()

    with jax.named_scope("grad_level_two"):
        skip_to_rows.wait()

        def grad_level(at):
            x = buf.level_two_rows[block(at, 64)].astype(F32)
            g = buf.grad_skip_rows[block(at, 64)].astype(F32)
            both = by_row(norm_back(x, g), C2)
            for row in range(2):
                where = pl.ds(pl.multiple_of(at * 32 + 128 * row, 32), 32)
                buf.right_p[where] = both[row].reshape(32, C2).astype(BF)

        loop(4, grad_level)

        def grad_mixed(at):
            buf.grad_mixed_two[:, block(at, 256)] = dot_nt(
                buf.right_p[0:256], weight.proj_two[block(at, 256)]
            ).astype(BF)

        loop(4, grad_mixed)

        def attend_two_back(at):
            places = [(2 * at + k, row) for k in range(2) for row in range(2)]
            units = []
            for pair, row in places:
                rows = slice(128 * row, 128 * row + 128)
                units.append(
                    operands_two(row, pair)
                    + [
                        buf.expo_two[pair * 2 + row],
                        buf.over_two[pair * 2 + row],
                        buf.mixed_two[rows, block(pair, 128)],
                        buf.grad_mixed_two[rows, block(pair, 128)],
                    ]
                )
            for (pair, row), found in zip(places, attend_back(units)):
                for third in range(3):
                    where = pl.ds(pl.multiple_of(C2 * third + pair * 128, 128), 128)
                    buf.right_q[128 * row : 128 * row + 128, where] = found[third]

        loop(4, attend_two_back)

    def turn(source, left, slot):
        first = c["core"] == 0
        for half in range(2):
            tokens_at = slice(128 * half, 128 * half + 128)
            groups = source[tokens_at].astype(F32).T.reshape(64, 2, 8, 128)
            mine = jnp.where(first, groups[:, 0], groups[:, 1])
            theirs = jnp.where(first, groups[:, 1], groups[:, 0])
            left[:, tokens_at] = mine.reshape(512, 128).astype(BF)
            buf.leave[slot, :, tokens_at] = theirs.reshape(512, 128).astype(BF)

    pair_copies = [
        remote(source, target, pair_send.at[k], pair_recv.at[k], device_of(moved(c, "core", 1)))
        for k, (source, target) in enumerate(
            (
                (buf.right_q.at[0:256], buf.right_q.at[256:512]),
                (buf.right_p.at[0:256], buf.right_p.at[256:512]),
                (buf.leave.at[0], buf.left_q.at[:, 256:512]),
                (buf.leave.at[1], buf.left_p.at[:, 256:512]),
            )
        )
    ]

    with jax.named_scope("grad_coarse"):
        pair_copies[0].start()
        pair_copies[1].start()

        def grad_normed_two(at):
            buf.grad_mixed_two[:, block(at, 256)] = dot_nt(
                buf.right_q[0:256], weight.qkv_two[block(at, 256)]
            ).astype(BF)

        loop(4, grad_normed_two)

        def grad_coarse(at):
            both = []
            for row in range(2):
                where = pl.ds(pl.multiple_of(at * 32 + 128 * row, 32), 32)
                g = norm_back(buf.wide[where], buf.grad_mixed_two[where].astype(F32))
                g = g.astype(BF).astype(F32) + buf.right_p[where].astype(F32)
                both.append(g.reshape(4, 8, C2))
            buf.grad_coarse_rows[block(at, 64)] = (
                jnp.stack(both, axis=1).reshape(64, C2).astype(BF)
            )

        loop(4, grad_coarse)
        grad_to_tile.start()

    with jax.named_scope("weight_gradients"):
        turn(buf.normed_two, buf.left_q, 0)
        pair_copies[2].start()
        turn(buf.mixed_two, buf.left_p, 1)
        pair_copies[3].start()
        for copy in pair_copies:
            copy.wait_recv()

        def put_total(zh, columns, top, low):
            width = top.shape[1]
            both = jnp.concatenate([top.reshape(32, 8, width), low.reshape(32, 8, width)], axis=1)
            reducer.total[zh, :, :, :, :, columns] = both.astype(BF).reshape(4, 2, 4, 16, width)

        def narrow_tile(at):
            right = jnp.concatenate(
                [buf.right_q[:, block(at, 128)], buf.right_q[:, block(at + 16, 128)]], axis=1
            )
            for zh in range(2):
                both = dot(buf.left_q[256 * zh : 256 * zh + 256], right)
                put_total(zh, block(at, 128), both[:, :128], both[:, 128:])

        def wide_tile(at):
            for zh in range(2):
                rows = slice(256 * zh, 256 * zh + 256)
                top = dot(buf.left_q[rows], buf.right_q[:, block(at, 256)])
                low = dot(buf.left_p[rows], buf.right_p[:, block(at - 4, 256)])
                put_total(zh, block(at, 256), top, low)

        for part, (start, stop, _) in enumerate(PARTS):
            middle = max(start, min(stop, 1024))
            if middle > start:
                loop((middle - start) // 128, lambda at: narrow_tile(at + start // 128))
            if stop > middle:
                loop((stop - middle) // 256, lambda at: wide_tile(at + middle // 256))
            reducer.start(part, 0)

    with jax.named_scope("grad_fine"):
        grad_to_tile.wait()

        def grad_grouped(at):
            buf.grouped[:, block(at, 256)] = dot_nt(
                buf.grad_coarse[...], weight.merge[block(at, 256)]
            ).astype(BF)

        loop(8, grad_grouped)

        def grad_pieces(at):
            g = norm_back(
                buf.fine[block(at, 16)].astype(F32), buf.grouped[block(at, 16)].astype(F32)
            )
            put_pieces(buf.spare, at, [g[:, C1 * k : C1 * k + C1] for k in range(4)])

        loop(16, grad_pieces)

        cotangent_again.wait()

        def grad_fine(at):
            buf.normed_one[block(at, 64)] = (
                joined_rows(buf.spare, at, C1) + buf.y_shift[block(at, 64)].astype(F32)
            ).astype(BF)

        loop(16, grad_fine)
        grads_in.pack(0)
        grads_in.pack(1)
        grads_in.start(range(4))

    with jax.named_scope("output"):
        level_to_tile.wait()

        def norm_level(at):
            x = buf.level_two[block(at, 64)].astype(F32)
            buf.coarse[block(at, 64)] = normalised(x)[0].astype(BF)

        coarse_to_rows.drain()
        loop(4, norm_level)

        for half in range(2):
            rows = slice(128 * half, 128 * half + 128)

            def unmerge(at):
                for low in range(2):
                    buf.wide[128 * low : 128 * low + 128, block(at, 256)] = dot(
                        buf.coarse[rows], weight.unmerge[:, block(at + 4 * low, 256)]
                    )

            loop(4, unmerge)

            def add_fine(at):
                fine = buf.fine[block(at + 8 * half, 16)].astype(F32)
                upper = jnp.concatenate(
                    [buf.wide[block(at, 16)], buf.wide[block(at + 8, 16)]], axis=1
                )
                total = fine + upper
                put_pieces(
                    buf.spare,
                    at + 8 * half,
                    [total[:, C1 * k : C1 * k + C1] for k in range(4)],
                )

            loop(8, add_fine)

        def write_output(at):
            buf.outgoing[block(at, 64)] = joined_rows(buf.spare, at, C1).astype(BF)

        loop(16, write_output)
        output_store.start()

    with jax.named_scope("grad_level_one"):

        def write_grads(at, rows):
            buf.grads[block(at, 64)] = rows.astype(BF)

        grads_in.wait(range(4))
        grads_in.assemble(0, write_grads)
        grads_in.assemble(1, write_grads)
        grads_in.drain()
        for half in range(2):
            rows = slice(512 * half, 512 * half + 512)

            def grad_mixed_one(at):
                buf.normed_one[rows, block(at, 256)] = dot_nt(
                    buf.grads[rows], weight.proj_one[block(at, 256)]
                ).astype(BF)

            loop(2, grad_mixed_one)

            def attend_group_back(at):
                group = at + 4 * half
                where = block(group, 128)
                units = []
                for pair in range(4):
                    at_unit = group * 4 + pair
                    units.append(
                        [buf.packed_one[where, lanes(third, pair)] for third in range(3)]
                        + [
                            buf.expo_one[at_unit],
                            buf.over_one[at_unit],
                            buf.mixed_one[where, lanes(0, pair)],
                            buf.normed_one[where, lanes(0, pair)],
                        ]
                    )
                for pair, found in enumerate(attend_back(units)):
                    for third in range(3):
                        buf.packed_one[where, lanes(third, pair)] = found[third]

            loop(4, attend_group_back)

            def grad_normed_one(at):
                buf.normed_one[rows, block(at, 256)] = dot_nt(
                    buf.packed_one[rows], weight.qkv_one[block(at, 256)]
                ).astype(BF)

            loop(2, grad_normed_one)

            def grad_window(at):
                where = block(at + 8 * half, 64)
                g = norm_back(
                    buf.window[where].astype(F32), buf.normed_one[where].astype(F32)
                )
                buf.y_shift[where] = (g + buf.grads[where].astype(F32)).astype(BF)

            loop(8, grad_window)
            grads_back.pack(half)
            grads_back.start((0, 1, 2) if half == 0 else (3,))
            for part in range(3):
                reducer.finish(part, half)
                reducer.start(part, half + 1)

    with jax.named_scope("grad_tokens"):
        output_store.wait()

        def write_tokens(at, rows):
            buf.outgoing[block(at, 64)] = rows.astype(BF)

        grads_back.wait((0, 1, 2))
        grads_back.assemble(0, write_tokens)
        grads_back.wait((3,))
        grads_back.assemble(1, write_tokens)
        grad_store.start()
        for part in range(3):
            store_folded(part, reducer.finish(part, 2), qkv_ref, proj_ref)

    tokens_in.drain()
    grads_back.drain()
    skip_to_rows.drain()
    level_to_tile.drain()
    grad_to_tile.drain()
    for copy in pair_copies:
        copy.wait_send()
    reducer.drain()
    grad_store.wait()


def hand_over(*refs):
    for source, target in zip(refs[:4], refs[4:]):
        target[...] = source[...]


def body(
    tokens, region, qkv_one, proj_one, merge_weight, qkv_two, proj_two, unmerge_weight, cotangent
):
    vmem = pl.BlockSpec(memory_space=pltpu.VMEM)
    anywhere = pl.BlockSpec(memory_space=pl.ANY)
    shapes = (
            jax.ShapeDtypeStruct((TOKENS, C1), BF),
            jax.ShapeDtypeStruct((TOKENS, C1), BF),
            jax.ShapeDtypeStruct((8, 3 * C2), F32),
            jax.ShapeDtypeStruct((8, C2), F32),
    )
    found = pl.pallas_call(
        whole_kernel,
        out_shape=shapes,
        in_specs=[vmem] + [anywhere] * 8,
        out_specs=(anywhere, anywhere, vmem, vmem),
        scratch_shapes=scratch_list(),
        compiler_params=pltpu.CompilerParams(
            collective_id=0, has_side_effects=True, vmem_limit_bytes=VMEM_LIMIT
        ),
    )(
        region.T,
        tokens.reshape(TOKENS, C1),
        cotangent.reshape(TOKENS, C1),
        unmerge_weight,
        qkv_one,
        proj_one,
        merge_weight,
        qkv_two,
        proj_two,
    )
    pieces = [
        pl.BlockSpec((TOKENS // 4, C1), lambda at: (at, 0)),
        pl.BlockSpec((TOKENS // 4, C1), lambda at: (at, 0)),
        pl.BlockSpec((8, 3 * C2 // 4), lambda at: (0, at)),
        pl.BlockSpec((8, C2 // 4), lambda at: (0, at)),
    ]
    output, grad_tokens, grad_qkv_two, grad_proj_two = pl.pallas_call(
        hand_over, grid=(4,), out_shape=shapes, in_specs=pieces, out_specs=pieces
    )(*found)
    shape = tokens.shape
    return output.reshape(shape), grad_tokens.reshape(shape), grad_qkv_two, grad_proj_two


def solution(mesh):
    return jax.shard_map(
        body,
        mesh=mesh,
        in_specs=(
            P("lat", "lon", None),
            P("lat", "lon"),
            P(),
            P(),
            P(),
            P(),
            P(),
            P(),
            P("lat", "lon", None),
        ),
        out_specs=(
            P("lat", "lon", None),
            P("lat", "lon", None),
            P(("lat", "lon"), None),
            P(("lat", "lon"), None),
        ),
        check_vma=False,
    )
```

profile of v0, /device:TPU:0, one launch (start us, length us, event | category | flops | bytes accessed | tf_op | source)
XLA Modules:
  0.0 120.0 jit_solution(1277139798058450136)
XLA Ops:
  0.6 115.5 %shard_map.120 = (bf16[1024,512]{1,0:T(8,128)(2,1)}, bf16[1024,512]{1,0:T(8,128)(2,1)}, f32[8,3072]{1,0:T(8,128)}, f32[8,1024]{1,0:T(8,128)}) custom-call(s32[16,64]{1,0:T(8,128)} %bitcast.7, bf16[1024,512]{1,0:T(8,128)(2,1)} %bitcast.5, bf16[1024,512]{1,0:T(8,128)(2,1)} %bitcast.6, bf16[1024,2048]{1,0:T(8,128)(2,1)} %refs_3_.1, bf16[512,1536]{1,0:T(8,128)(2,1)} %refs_4_.1, ...), custom_call_target="tpu_custom_call" | custom-call | tf_op jit(solution)/shard_map/pallas_call | solution.py:994
  116.2 3.8 %shard_map.121 = (bf16[1024,512]{1,0:T(8,128)(2,1)}, bf16[1024,512]{1,0:T(8,128)(2,1)}, f32[8,3072]{1,0:T(8,128)}, f32[8,1024]{1,0:T(8,128)}) custom-call(bf16[1024,512]{1,0:T(8,128)(2,1)} %get-tuple-element.12.refs_0_, bf16[1024,512]{1,0:T(8,128)(2,1)} %get-tuple-element.13.refs_1_, f32[8,3072]{1,0:T(8,128)} %get-tuple-element.14.refs_2_, ...), custom_call_target="tpu_custom_call" | custom-call | tf_op jit(solution)/shard_map/pallas_call | solution.py:1020
where the time goes:
time: 121 us; the launch traced here: 120 us
  Pallas kernels  119 us (98%)
    pallas_call x1, Pallas kernels, body(): pl.pallas_call(whole_kernel, out_shape=shapes, in_specs=[vmem] + [anywher...  116 us
    pallas_call x1, Pallas kernels, body(): pl.pallas_call(hand_over, grid=(4,), out_shape=shapes, in_specs=pieces, o...  3.79 us

commit v1 on v0

--- a/solution.py
+++ b/solution.py
@@ -16,6 +16,7 @@
 TOKENS, C1, C2 = 1024, 512, 1024
 COARSE = 256
 LONS, LATS = 16, 8
+DENSE, HEADS, TILES = 4, 1, 1
 
 FOLD = 2048
 PARTS = ((0, 640, ("x", "y", "z")), (640, 1280, ("y", "z", "x")), (1280, 2048, ("z", "x", "y")))
@@ -163,12 +164,15 @@
     return pl.ds(pl.multiple_of(at * size, size), size)
 
 
-def loop(count, body):
-    def step(at, carry):
-        body(at)
+def loop(count, body, most=4):
+    size = max(k for k in range(1, most + 1) if count % k == 0)
+
+    def turn(at, carry):
+        for k in range(size):
+            body(at * size + k)
         return carry
 
-    lax.fori_loop(0, count, step, 0)
+    lax.fori_loop(0, count // size, turn, 0)
 
 
 def dot(a, b):
@@ -326,7 +330,7 @@
                 rows = self.field[pl.ds(pl.multiple_of(at * 64 + self.first, 64), 64)]
                 write(at + 1, put_columns(rows.astype(F32), self.columns[block(at + 1, 16)]))
 
-            loop(7 if part else 8, patch)
+            loop(7 if part else 8, patch, 8)
         else:
             if part == 0:
                 write(15, put_columns(self.rows[...].astype(F32), self.columns[240:256]))
@@ -336,7 +340,7 @@
                 rows = self.field[block(at + 1, 64)]
                 write(at, put_columns(rows.astype(F32), self.columns[block(at, 16)]))
 
-            loop(8 if part else 7, patch)
+            loop(8 if part else 7, patch, 8)
 
 
 def halo_scratch():
@@ -367,15 +371,15 @@
         )
 
     def start(self):
-        loop(15, lambda at: self.copy(at + 1).start())
+        loop(15, lambda at: self.copy(at + 1).start(), 1)
         lon = lax.axis_index("lon")
         self.target[block(lon, 16)] = self.source[block(lon, 16)]
 
     def wait(self):
-        loop(15, lambda at: self.copy(at + 1).wait_recv())
+        loop(15, lambda at: self.copy(at + 1).wait_recv(), 1)
 
     def drain(self):
-        loop(15, lambda at: self.copy(at + 1).wait_send())
+        loop(15, lambda at: self.copy(at + 1).wait_send(), 1)
 
 
 def spread_lanes(ref, at, rows):
@@ -429,14 +433,12 @@
     over_one=((32, 128, 128), BF),
     mixed_one=((TOKENS, C1), BF),
     y_shift=((TOKENS, C1), BF),
-    grads=((TOKENS, C1), BF),
     outgoing=((TOKENS, C1), BF),
     fine=((COARSE, 4 * C1), BF),
     spare=((4, TOKENS, 128), F32),
     grouped=((COARSE, 4 * C1), BF),
     coarse=((COARSE, C2), BF),
     coarse_rows=((COARSE, C2), BF),
-    grad_skip=((COARSE, C2), BF),
     grad_skip_rows=((COARSE, C2), BF),
     normed_two=((COARSE, C2), BF),
     packed_two=((COARSE, 3 * C2), BF),
@@ -527,7 +529,7 @@
     fine_back = Halo(buf.y_shift, halos[1], -1)
     grads_in = Halo(buf.normed_one, halos[2], 1)
     grads_back = Halo(buf.y_shift, halos[3], -1)
-    skip_to_rows = Rows(buf.grad_skip, buf.grad_skip_rows, row_sems[0])
+    skip_to_rows = Rows(buf.grad_mixed_two, buf.grad_skip_rows, row_sems[0])
     coarse_to_rows = Rows(buf.coarse, buf.coarse_rows, row_sems[1])
     level_to_tile = Rows(buf.level_two_rows, buf.level_two, row_sems[2])
     grad_to_tile = Rows(buf.grad_coarse_rows, buf.grad_coarse, row_sems[3])
@@ -553,15 +555,6 @@
             ).astype(BF)
 
         loop(16, group_cotangent)
-        loads.unmerge.wait()
-
-        def grad_skip(at):
-            buf.grad_skip[:, block(at, 256)] = dot_nt(
-                buf.grouped[...], weight.unmerge[block(at, 256)]
-            ).astype(BF)
-
-        loop(4, grad_skip)
-        skip_to_rows.start()
 
     def lanes(third, pair):
         return slice(C1 * third + 128 * pair, C1 * third + 128 * pair + 128)
@@ -587,7 +580,7 @@
                     buf.normed_one[rows], weight.qkv_one[:, block(at, 256)]
                 ).astype(BF)
 
-            loop(6, project)
+            loop(6, project, DENSE)
 
             def attend_group(at):
                 group = at + 4 * half
@@ -601,7 +594,7 @@
                     buf.expo_one[at_unit], buf.over_one[at_unit], mixed = found
                     buf.mixed_one[where, lanes(0, pair)] = mixed
 
-            loop(4, attend_group)
+            loop(4, attend_group, HEADS)
 
             def add_tokens(at):
                 columns = block(at, 256)
@@ -610,11 +603,21 @@
                     + dot(buf.mixed_one[rows], weight.proj_one[:, columns])
                 ).astype(BF)
 
-            loop(2, add_tokens)
+            loop(2, add_tokens, DENSE)
             fine_back.pack(half)
             fine_back.start((0, 1, 2) if half == 0 else (3,))
 
     with jax.named_scope("merge"):
+        loads.unmerge.wait()
+
+        def grad_skip(at):
+            buf.grad_mixed_two[:, block(at, 256)] = dot_nt(
+                buf.grouped[...], weight.unmerge[block(at, 256)]
+            ).astype(BF)
+
+        loop(4, grad_skip, DENSE)
+        skip_to_rows.start()
+
         def write_fine(at, rows):
             spread_lanes(buf.spare, at, rows.astype(BF).astype(F32))
 
@@ -637,7 +640,7 @@
                 buf.grouped[...], weight.merge[:, columns]
             ).astype(BF)
 
-        loop(4, merge)
+        loop(4, merge, DENSE)
         coarse_to_rows.start()
         fine_back.drain()
         cotangent_again.start()
@@ -663,7 +666,7 @@
                 buf.normed_two[...], weight.qkv_two[:, columns]
             ).astype(BF)
 
-        loop(12, project_two)
+        loop(12, project_two, DENSE)
 
         def operands_two(row, pair):
             rows = slice(128 * row, 128 * row + 128)
@@ -680,7 +683,7 @@
                 buf.expo_two[at_unit], buf.over_two[at_unit], mixed = found
                 buf.mixed_two[128 * row : 128 * row + 128, block(pair, 128)] = mixed
 
-        loop(4, attend_two)
+        loop(4, attend_two, HEADS)
 
         def add_coarse(at):
             columns = block(at, 256)
@@ -691,7 +694,7 @@
                 .astype(BF)
             )
 
-        loop(4, add_coarse)
+        loop(4, add_coarse, DENSE)
         level_to_tile.start()
 
     with jax.named_scope("grad_level_two"):
@@ -706,13 +709,14 @@
                 buf.right_p[where] = both[row].reshape(32, C2).astype(BF)
 
         loop(4, grad_level)
+        skip_to_rows.drain()
 
         def grad_mixed(at):
             buf.grad_mixed_two[:, block(at, 256)] = dot_nt(
                 buf.right_p[0:256], weight.proj_two[block(at, 256)]
             ).astype(BF)
 
-        loop(4, grad_mixed)
+        loop(4, grad_mixed, DENSE)
 
         def attend_two_back(at):
             places = [(2 * at + k, row) for k in range(2) for row in range(2)]
@@ -733,7 +737,7 @@
                     where = pl.ds(pl.multiple_of(C2 * third + pair * 128, 128), 128)
                     buf.right_q[128 * row : 128 * row + 128, where] = found[third]
 
-        loop(4, attend_two_back)
+        loop(4, attend_two_back, HEADS)
 
     def turn(source, left, slot):
         first = c["core"] == 0
@@ -766,7 +770,7 @@
                 buf.right_q[0:256], weight.qkv_two[block(at, 256)]
             ).astype(BF)
 
-        loop(4, grad_normed_two)
+        loop(4, grad_normed_two, DENSE)
 
         def grad_coarse(at):
             both = []
@@ -813,9 +817,9 @@
         for part, (start, stop, _) in enumerate(PARTS):
             middle = max(start, min(stop, 1024))
             if middle > start:
-                loop((middle - start) // 128, lambda at: narrow_tile(at + start // 128))
+                loop((middle - start) // 128, lambda at: narrow_tile(at + start // 128), TILES)
             if stop > middle:
-                loop((stop - middle) // 256, lambda at: wide_tile(at + middle // 256))
+                loop((stop - middle) // 256, lambda at: wide_tile(at + middle // 256), TILES)
             reducer.start(part, 0)
 
     with jax.named_scope("grad_fine"):
@@ -826,7 +830,7 @@
                 buf.grad_coarse[...], weight.merge[block(at, 256)]
             ).astype(BF)
 
-        loop(8, grad_grouped)
+        loop(8, grad_grouped, DENSE)
 
         def grad_pieces(at):
             g = norm_back(
@@ -867,7 +871,7 @@
                         buf.coarse[rows], weight.unmerge[:, block(at + 4 * low, 256)]
                     )
 
-            loop(4, unmerge)
+            loop(4, unmerge, DENSE)
 
             def add_fine(at):
                 fine = buf.fine[block(at + 8 * half, 16)].astype(F32)
@@ -892,7 +896,7 @@
     with jax.named_scope("grad_level_one"):
 
         def write_grads(at, rows):
-            buf.grads[block(at, 64)] = rows.astype(BF)
+            buf.y_shift[block(at, 64)] = rows.astype(BF)
 
         grads_in.wait(range(4))
         grads_in.assemble(0, write_grads)
@@ -903,10 +907,10 @@
 
             def grad_mixed_one(at):
                 buf.normed_one[rows, block(at, 256)] = dot_nt(
-                    buf.grads[rows], weight.proj_one[block(at, 256)]
+                    buf.y_shift[rows], weight.proj_one[block(at, 256)]
                 ).astype(BF)
 
-            loop(2, grad_mixed_one)
+            loop(2, grad_mixed_one, DENSE)
 
             def attend_group_back(at):
                 group = at + 4 * half
@@ -927,21 +931,21 @@
                     for third in range(3):
                         buf.packed_one[where, lanes(third, pair)] = found[third]
 
-            loop(4, attend_group_back)
+            loop(4, attend_group_back, HEADS)
 
             def grad_normed_one(at):
                 buf.normed_one[rows, block(at, 256)] = dot_nt(
                     buf.packed_one[rows], weight.qkv_one[block(at, 256)]
                 ).astype(BF)
 
-            loop(2, grad_normed_one)
+            loop(2, grad_normed_one, DENSE)
 
             def grad_window(at):
                 where = block(at + 8 * half, 64)
                 g = norm_back(
                     buf.window[where].astype(F32), buf.normed_one[where].astype(F32)
                 )
-                buf.y_shift[where] = (g + buf.grads[where].astype(F32)).astype(BF)
+                buf.y_shift[where] = (g + buf.y_shift[where].astype(F32)).astype(BF)
 
             loop(8, grad_window)
             grads_back.pack(half)
@@ -966,7 +970,6 @@
 
     tokens_in.drain()
     grads_back.drain()
-    skip_to_rows.drain()
     level_to_tile.drain()
     grad_to_tile.drain()
     for copy in pair_copies:

time: 121 us -> 106 us (0.88)
  Pallas kernels: 119 us -> 104 us
    pallas_call x1, Pallas kernels: 116 us -> 99.8 us  [body(): pl.pallas_call(whole_kernel, out_shape=shapes, in_specs=[vmem] + [anywher...]
where the time goes in v1:
time: 106 us; the launch traced here: 104 us
  Pallas kernels  104 us (98%)
    pallas_call x1, Pallas kernels, body(): pl.pallas_call(whole_kernel, out_shape=shapes, in_specs=[vmem] + [anywher...  99.8 us
    pallas_call x1, Pallas kernels, body(): pl.pallas_call(hand_over, grid=(4,), out_shape=shapes, in_specs=pieces, o...  3.79 us

profile of v1, /device:TPU:0, one launch (start us, length us, event | category | flops | bytes accessed | tf_op | source)
XLA Modules:
  0.0 104.4 jit_solution(537108512871729576)
XLA Ops:
  0.6 99.8 %shard_map.120 = (bf16[1024,512]{1,0:T(8,128)(2,1)}, bf16[1024,512]{1,0:T(8,128)(2,1)}, f32[8,3072]{1,0:T(8,128)}, f32[8,1024]{1,0:T(8,128)}) custom-call(s32[16,64]{1,0:T(8,128)} %bitcast.7, bf16[1024,512]{1,0:T(8,128)(2,1)} %bitcast.5, bf16[1024,512]{1,0:T(8,128)(2,1)} %bitcast.6, bf16[1024,2048]{1,0:T(8,128)(2,1)} %refs_3_.1, bf16[512,1536]{1,0:T(8,128)(2,1)} %refs_4_.1, ...), custom_call_target="tpu_custom_call" | custom-call | tf_op jit(solution)/shard_map/pallas_call | solution.py:997
  100.4 3.8 %shard_map.121 = (bf16[1024,512]{1,0:T(8,128)(2,1)}, bf16[1024,512]{1,0:T(8,128)(2,1)}, f32[8,3072]{1,0:T(8,128)}, f32[8,1024]{1,0:T(8,128)}) custom-call(bf16[1024,512]{1,0:T(8,128)(2,1)} %get-tuple-element.12.refs_0_, bf16[1024,512]{1,0:T(8,128)(2,1)} %get-tuple-element.13.refs_1_, f32[8,3072]{1,0:T(8,128)} %get-tuple-element.14.refs_2_, ...), custom_call_target="tpu_custom_call" | custom-call | tf_op jit(solution)/shard_map/pallas_call | solution.py:1023

commit v2 on v1

--- a/solution.py
+++ b/solution.py
@@ -84,14 +84,15 @@
             shapes.append(pltpu.VMEM((3,) + sizes(labels) + (16, stop - start), BF))
             if step < 2:
                 shapes.append(pltpu.VMEM(sizes(labels) + (16, stop - start), BF))
-    return shapes + [pltpu.SemaphoreType.DMA((3, 3, 3)), pltpu.SemaphoreType.DMA((3, 3, 3))]
+    shapes += [pltpu.SemaphoreType.DMA((3, 3, 3)), pltpu.SemaphoreType.DMA((3, 3, 3))]
+    return shapes + [pltpu.SemaphoreType.DMA((3, 6)), pltpu.SemaphoreType.DMA((3, 6))]
 
 
 class Reducer:
     def __init__(self, scratch):
         self.total = scratch[0]
         self.slots = [scratch[1 + 5 * p : 6 + 5 * p] for p in range(3)]
-        self.send_sem, self.recv_sem = scratch[16], scratch[17]
+        self.send_sem, self.recv_sem, self.ring_send, self.ring_recv = scratch[16:]
         self.c = coordinates()
 
     def source(self, part, step):
@@ -120,12 +121,60 @@
             )
         return found
 
+    def ring(self, part):
+        start, stop, order = PARTS[part]
+        axis, width = order[0], stop - start
+        cut = width // 256 * 128
+        halves = ((0, cut), (cut, width - cut))
+        after, before, opposite = (moved(self.c, axis, by) for by in (1, 3, 2))
+        every = (slice(None),) * len(drop(LABELS, axis))
+
+        def mine(owner, half):
+            at, size = halves[half]
+            return self.total.at[pick(LABELS, axis, owner) + (slice(None), pl.ds(start + at, size))]
+
+        def slot(which, half):
+            at, size = halves[half]
+            return self.slots[part][0].at[(which,) + every + (slice(None), pl.ds(at, size))]
+
+        plan = (
+            (mine(opposite, 0), slot(2, 0), after),
+            (mine(opposite, 1), slot(2, 1), before),
+            (mine(after, 1), slot(0, 1), after),
+            (mine(before, 0), slot(1, 0), before),
+            (slot(2, 0), slot(0, 0), after),
+            (slot(2, 1), slot(1, 1), before),
+        )
+        copies = [
+            remote(source, target, self.ring_send.at[part, k], self.ring_recv.at[part, k], device_of(device))
+            for k, (source, target, device) in enumerate(plan)
+        ]
+        return copies, halves, (after, before)
+
     def start(self, part, step):
-        for copy in self.copies(part, step):
+        copies = self.copies(part, step) if step else self.ring(part)[0][:4]
+        for copy in copies:
             copy.start()
 
+    def pass_on(self, part):
+        copies, halves, owners = self.ring(part)
+        start, _, order = PARTS[part]
+        left = drop(LABELS, order[0])
+        passed = self.slots[part][0]
+        for half, (at, size) in enumerate(halves):
+            copies[half].wait_recv()
+            for place in itertools.product(*[range(count) for count in sizes(left)]):
+                where = {**owners[half], **dict(zip(left, place))}
+                own = self.total[
+                    tuple(where[label] for label in LABELS) + (slice(None), slice(start + at, start + at + size))
+                ]
+                here = (2,) + place + (slice(None), slice(at, at + size))
+                passed[here] = (passed[here].astype(F32) + own.astype(F32)).astype(BF)
+            copies[4 + half].start()
+
     def finish(self, part, step):
-        for copy in self.copies(part, step):
+        copies = self.copies(part, step) if step else self.ring(part)[0][2:]
+        for copy in copies:
             copy.wait_recv()
         axis = PARTS[part][2][step]
         labels, source, rest = self.source(part, step)
@@ -136,7 +185,7 @@
             where.update({k: self.c[k] for k in labels if k not in where})
             own = source[tuple(where[label] for label in labels) + rest].astype(F32)
             summed = own
-            for slot in range(3):
+            for slot in range(3 if step else 2):
                 summed = summed + arrived[(slot,) + place].astype(F32)
             if step == 2:
                 return summed
@@ -144,7 +193,9 @@
 
     def drain(self):
         for part in range(3):
-            for step in range(3):
+            for copy in self.ring(part)[0]:
+                copy.wait_send()
+            for step in range(1, 3):
                 for copy in self.copies(part, step):
                     copy.wait_send()
 
@@ -370,10 +421,20 @@
             (lat, to),
         )
 
-    def start(self):
-        loop(15, lambda at: self.copy(at + 1).start(), 1)
+    def start_to(self, to):
         lon = lax.axis_index("lon")
-        self.target[block(lon, 16)] = self.source[block(lon, 16)]
+        by = (to - lon + LONS) % LONS
+
+        @pl.when(by != 0)
+        def _():
+            self.copy(by).start()
+
+        @pl.when(by == 0)
+        def _():
+            self.target[block(lon, 16)] = self.source[block(lon, 16)]
+
+    def start(self, half):
+        loop(8, lambda at: self.start_to(at + 8 * half), 1)
 
     def wait(self):
         loop(15, lambda at: self.copy(at + 1).wait_recv(), 1)
@@ -616,32 +677,36 @@
             ).astype(BF)
 
         loop(4, grad_skip, DENSE)
-        skip_to_rows.start()
+        skip_to_rows.start(0)
+        skip_to_rows.start(1)
 
         def write_fine(at, rows):
             spread_lanes(buf.spare, at, rows.astype(BF).astype(F32))
-
-        fine_back.wait((0, 1, 2))
-        fine_back.assemble(0, write_fine)
-        fine_back.wait((3,))
-        fine_back.assemble(1, write_fine)
 
         def group_fine(at):
             whole = jnp.concatenate(fine_pieces(buf.spare, at), axis=1)
             buf.fine[block(at, 16)] = whole.astype(BF)
             buf.grouped[block(at, 16)] = normalised(whole)[0].astype(BF)
 
-        loop(16, group_fine)
+        fine_back.wait((0, 1, 2))
+        fine_back.assemble(0, write_fine)
+        loop(8, lambda at: group_fine((at + 15) % 16))
+        fine_back.wait((3,))
+        fine_back.assemble(1, write_fine)
+        loop(8, lambda at: group_fine(at + 7))
         loads.merge.wait()
 
-        def merge(at):
-            columns = block(at, 256)
-            buf.coarse[:, columns] = dot(
-                buf.grouped[...], weight.merge[:, columns]
-            ).astype(BF)
-
-        loop(4, merge, DENSE)
-        coarse_to_rows.start()
+        for half in range(2):
+            rows = slice(128 * half, 128 * half + 128)
+
+            def merge(at):
+                columns = block(at, 256)
+                buf.coarse[rows, columns] = dot(
+                    buf.grouped[rows], weight.merge[:, columns]
+                ).astype(BF)
+
+            loop(4, merge, DENSE)
+            coarse_to_rows.start(half)
         fine_back.drain()
         cotangent_again.start()
 
@@ -695,7 +760,20 @@
             )
 
         loop(4, add_coarse, DENSE)
-        level_to_tile.start()
+        level_to_tile.start(0)
+        level_to_tile.start(1)
+
+    pair_copies = [
+        remote(source, target, pair_send.at[k], pair_recv.at[k], device_of(moved(c, "core", 1)))
+        for k, (source, target) in enumerate(
+            (
+                (buf.right_q.at[0:256], buf.right_q.at[256:512]),
+                (buf.right_p.at[0:256], buf.right_p.at[256:512]),
+                (buf.leave.at[0], buf.left_q.at[:, 256:512]),
+                (buf.leave.at[1], buf.left_p.at[:, 256:512]),
+            )
+        )
+    ]
 
     with jax.named_scope("grad_level_two"):
         skip_to_rows.wait()
@@ -709,6 +787,7 @@
                 buf.right_p[where] = both[row].reshape(32, C2).astype(BF)
 
         loop(4, grad_level)
+        pair_copies[1].start()
         skip_to_rows.drain()
 
         def grad_mixed(at):
@@ -749,21 +828,8 @@
             left[:, tokens_at] = mine.reshape(512, 128).astype(BF)
             buf.leave[slot, :, tokens_at] = theirs.reshape(512, 128).astype(BF)
 
-    pair_copies = [
-        remote(source, target, pair_send.at[k], pair_recv.at[k], device_of(moved(c, "core", 1)))
-        for k, (source, target) in enumerate(
-            (
-                (buf.right_q.at[0:256], buf.right_q.at[256:512]),
-                (buf.right_p.at[0:256], buf.right_p.at[256:512]),
-                (buf.leave.at[0], buf.left_q.at[:, 256:512]),
-                (buf.leave.at[1], buf.left_p.at[:, 256:512]),
-            )
-        )
-    ]
-
     with jax.named_scope("grad_coarse"):
         pair_copies[0].start()
-        pair_copies[1].start()
 
         def grad_normed_two(at):
             buf.grad_mixed_two[:, block(at, 256)] = dot_nt(
@@ -783,8 +849,9 @@
                 jnp.stack(both, axis=1).reshape(64, C2).astype(BF)
             )
 
-        loop(4, grad_coarse)
-        grad_to_tile.start()
+        for half in range(2):
+            loop(2, lambda at: grad_coarse(at + 2 * half))
+            grad_to_tile.start(half)
 
     with jax.named_scope("weight_gradients"):
         turn(buf.normed_two, buf.left_q, 0)
@@ -831,6 +898,8 @@
             ).astype(BF)
 
         loop(8, grad_grouped, DENSE)
+        for part in range(3):
+            reducer.pass_on(part)
 
         def grad_pieces(at):
             g = norm_back(
@@ -898,11 +967,11 @@
         def write_grads(at, rows):
             buf.y_shift[block(at, 64)] = rows.astype(BF)
 
-        grads_in.wait(range(4))
-        grads_in.assemble(0, write_grads)
-        grads_in.assemble(1, write_grads)
-        grads_in.drain()
         for half in range(2):
+            grads_in.wait((3,) if half else (0, 1, 2))
+            grads_in.assemble(half, write_grads)
+            if half:
+                grads_in.drain()
             rows = slice(512 * half, 512 * half + 512)
 
             def grad_mixed_one(at):
@@ -932,6 +1001,9 @@
                         buf.packed_one[where, lanes(third, pair)] = found[third]
 
             loop(4, attend_group_back, HEADS)
+            for part in range(3):
+                reducer.finish(part, half)
+                reducer.start(part, half + 1)
 
             def grad_normed_one(at):
                 buf.normed_one[rows, block(at, 256)] = dot_nt(
@@ -950,9 +1022,6 @@
             loop(8, grad_window)
             grads_back.pack(half)
             grads_back.start((0, 1, 2) if half == 0 else (3,))
-            for part in range(3):
-                reducer.finish(part, half)
-                reducer.start(part, half + 1)
 
     with jax.named_scope("grad_tokens"):
         output_store.wait()
@@ -1015,13 +1084,13 @@
         proj_two,
     )
     pieces = [
-        pl.BlockSpec((TOKENS // 4, C1), lambda at: (at, 0)),
-        pl.BlockSpec((TOKENS // 4, C1), lambda at: (at, 0)),
-        pl.BlockSpec((8, 3 * C2 // 4), lambda at: (0, at)),
-        pl.BlockSpec((8, C2 // 4), lambda at: (0, at)),
+        pl.BlockSpec((TOKENS // 2, C1), lambda at: (at, 0)),
+        pl.BlockSpec((TOKENS // 2, C1), lambda at: (at, 0)),
+        pl.BlockSpec((8, 3 * C2 // 2), lambda at: (0, at)),
+        pl.BlockSpec((8, C2 // 2), lambda at: (0, at)),
     ]
     output, grad_tokens, grad_qkv_two, grad_proj_two = pl.pallas_call(
-        hand_over, grid=(4,), out_shape=shapes, in_specs=pieces, out_specs=pieces
+        hand_over, grid=(2,), out_shape=shapes, in_specs=pieces, out_specs=pieces
     )(*found)
     shape = tokens.shape
     return output.reshape(shape), grad_tokens.reshape(shape), grad_qkv_two, grad_proj_two

time: 106 us -> 99.2 us (0.936)
  Pallas kernels: 104 us -> 97.1 us
    pallas_call x1, Pallas kernels: 99.8 us -> 94.4 us  [body(): pl.pallas_call(whole_kernel, out_shape=shapes, in_specs=[vmem] + [anywher...]
    pallas_call x1, Pallas kernels: 3.79 us -> 2.64 us  [body(): pl.pallas_call(hand_over, grid=(2,), out_shape=shapes, in_specs=pieces, o...]
where the time goes in v2:
time: 99.2 us; the launch traced here: 97.9 us
  Pallas kernels  97.1 us (98%)
    pallas_call x1, Pallas kernels, body(): pl.pallas_call(whole_kernel, out_shape=shapes, in_specs=[vmem] + [anywher...  94.4 us
    pallas_call x1, Pallas kernels, body(): pl.pallas_call(hand_over, grid=(2,), out_shape=shapes, in_specs=pieces, o...  2.64 us

profile of v2, /device:TPU:0, one launch (start us, length us, event | category | flops | bytes accessed | tf_op | source)
XLA Modules:
  0.0 97.9 jit_solution(13239723228493406194)
XLA Ops:
  0.6 94.4 %shard_map.120 = (bf16[1024,512]{1,0:T(8,128)(2,1)}, bf16[1024,512]{1,0:T(8,128)(2,1)}, f32[8,3072]{1,0:T(8,128)}, f32[8,1024]{1,0:T(8,128)}) custom-call(s32[16,64]{1,0:T(8,128)} %bitcast.7, bf16[1024,512]{1,0:T(8,128)(2,1)} %bitcast.5, bf16[1024,512]{1,0:T(8,128)(2,1)} %bitcast.6, bf16[1024,2048]{1,0:T(8,128)(2,1)} %refs_3_.1, bf16[512,1536]{1,0:T(8,128)(2,1)} %refs_4_.1, ...), custom_call_target="tpu_custom_call" | custom-call | tf_op jit(solution)/shard_map/pallas_call | solution.py:1066
  95.1 2.6 %shard_map.121 = (bf16[1024,512]{1,0:T(8,128)(2,1)}, bf16[1024,512]{1,0:T(8,128)(2,1)}, f32[8,3072]{1,0:T(8,128)}, f32[8,1024]{1,0:T(8,128)}) custom-call(bf16[1024,512]{1,0:T(8,128)(2,1)} %get-tuple-element.12.refs_0_, bf16[1024,512]{1,0:T(8,128)(2,1)} %get-tuple-element.13.refs_1_, f32[8,3072]{1,0:T(8,128)} %get-tuple-element.14.refs_2_, ...), custom_call_target="tpu_custom_call" | custom-call | tf_op jit(solution)/shard_map/pallas_call | solution.py:1092

commit v3 on v2

--- a/solution.py
+++ b/solution.py
@@ -16,7 +16,7 @@
 TOKENS, C1, C2 = 1024, 512, 1024
 COARSE = 256
 LONS, LATS = 16, 8
-DENSE, HEADS, TILES = 4, 1, 1
+DENSE, HEADS, TILES = 4, 1, 5
 
 FOLD = 2048
 PARTS = ((0, 640, ("x", "y", "z")), (640, 1280, ("y", "z", "x")), (1280, 2048, ("z", "x", "y")))

time: 99.2 us -> 98.1 us (0.989)
  no operation moved by 1% of the time
where the time goes in v3:
time: 98.1 us; the launch traced here: 97 us
  Pallas kernels  96.2 us (98%)
    pallas_call x1, Pallas kernels, body(): pl.pallas_call(whole_kernel, out_shape=shapes, in_specs=[vmem] + [anywher...  93.6 us
    pallas_call x1, Pallas kernels, body(): pl.pallas_call(hand_over, grid=(2,), out_shape=shapes, in_specs=pieces, o...  2.64 us

profile of v3, /device:TPU:0, one launch (start us, length us, event | category | flops | bytes accessed | tf_op | source)
XLA Modules:
  0.0 97.0 jit_solution(5219277918264268826)
XLA Ops:
  0.6 93.6 %shard_map.120 = (bf16[1024,512]{1,0:T(8,128)(2,1)}, bf16[1024,512]{1,0:T(8,128)(2,1)}, f32[8,3072]{1,0:T(8,128)}, f32[8,1024]{1,0:T(8,128)}) custom-call(s32[16,64]{1,0:T(8,128)} %bitcast.7, bf16[1024,512]{1,0:T(8,128)(2,1)} %bitcast.5, bf16[1024,512]{1,0:T(8,128)(2,1)} %bitcast.6, bf16[1024,2048]{1,0:T(8,128)(2,1)} %refs_3_.1, bf16[512,1536]{1,0:T(8,128)(2,1)} %refs_4_.1, ...), custom_call_target="tpu_custom_call" | custom-call | tf_op jit(solution)/shard_map/pallas_call | solution.py:1066
  94.2 2.6 %shard_map.121 = (bf16[1024,512]{1,0:T(8,128)(2,1)}, bf16[1024,512]{1,0:T(8,128)(2,1)}, f32[8,3072]{1,0:T(8,128)}, f32[8,1024]{1,0:T(8,128)}) custom-call(bf16[1024,512]{1,0:T(8,128)(2,1)} %get-tuple-element.12.refs_0_, bf16[1024,512]{1,0:T(8,128)(2,1)} %get-tuple-element.13.refs_1_, f32[8,3072]{1,0:T(8,128)} %get-tuple-element.14.refs_2_, ...), custom_call_target="tpu_custom_call" | custom-call | tf_op jit(solution)/shard_map/pallas_call | solution.py:1092
